TPU v7x, 512 devices: a whole 4x4x16 slice. The times are simulated.
512 devices in a mesh: row: 16 (over x, z_lo), col: 32 (over y, z_hi, core).
Axes of the slice: x: 4, y: 4, z: 16 (z_hi: 4, z_lo: 4; z = z_hi * 4 + z_lo), core: 2. Of those that a mesh axis runs over, the one named last changes fastest.
Arguments:
- attn: bfloat16 [2048, 16384], P('col', 'row'), may hold values from -6 to 6
- w_out: bfloat16 [16384, 16384], P('row', 'col'), may hold values from -0.046875 to 0.046875
- resid: bfloat16 [2048, 16384], P('row', 'col'), may hold values from -6 to 6
- gain: float32 [16384], P('col'), may hold values from 0.3 to 3
Outputs:
- stream: bfloat16 [2048, 16384], P('row', 'col')
- gram: float32 [16384, 16384], P('row', 'col')
All inputs are finite; a program needn't handle non-finite values.
Results may differ from a plain program's by a relative error of at most 0.0034.
Values may be sent and summed in bfloat16 or wider, within the bound.
A program may use at most 64 MiB of HBM per device.

v0:
```python
import jax
import jax.numpy as jnp
from jax import lax
from jax.sharding import PartitionSpec as P

D = 16384


def spread(block, axis, holder):
    block = jnp.where(lax.axis_index(axis) == holder, block, jnp.zeros_like(block))
    return lax.psum(block, axis)


def local(attn, w_out, resid, gain):
    gathered = lax.all_gather(attn, "col", axis=0, tiled=True)
    partial_sums = jnp.dot(gathered, w_out, preferred_element_type=jnp.float32)
    proj = lax.psum_scatter(partial_sums, "row", scatter_dimension=0, tiled=True)
    summed = resid.astype(jnp.float32) + proj
    stream = summed.astype(jnp.bfloat16)
    squares = lax.psum(jnp.sum(summed * summed, axis=1, keepdims=True), "col")
    normed = (summed * gain[None, :] * lax.rsqrt(squares / D + 1e-05)).astype(jnp.bfloat16)
    col_data = lax.all_gather(normed, "row", axis=0, tiled=True)
    ratio = lax.axis_size("col") // lax.axis_size("row")
    row_index = lax.axis_index("row")
    col_index = lax.axis_index("col")
    pieces = []
    for offset in range(ratio):
        pieces.append(spread(col_data, "col", row_index * ratio + offset))
    row_data = jnp.concatenate(pieces, axis=1)
    block_rows = row_data.shape[1]
    block_cols = col_data.shape[1]
    total_tokens = col_data.shape[0]
    row_start = row_index * block_rows
    col_start = col_index * block_cols
    tile = lax.dot_general(
        row_data, col_data, (((0,), (0,)), ((), ())), preferred_element_type=jnp.float32
    )
    tile = tile * (2.0 / total_tokens)
    rows_idx = row_start + jnp.arange(block_rows, dtype=jnp.int32)[:, None]
    cols_idx = col_start + jnp.arange(block_cols, dtype=jnp.int32)[None, :]
    gram = jnp.where(cols_idx >= rows_idx, tile, jnp.zeros_like(tile))
    return (stream, gram)


def solution(mesh):
    placed = (P("col", "row"), P("row", "col"), P("row", "col"), P("col"))
    return jax.shard_map(
        local,
        mesh=mesh,
        in_specs=placed,
        out_specs=(P("row", "col"), P("row", "col")),
        check_vma=False,
    )
```

profile of v0, /device:TPU:1, one launch (start us, length us, event | category | flops | bytes accessed | tf_op | source)
XLA Modules:
  0.0 788.8 jit_solution(4903133360528197205)
XLA Ops:
  7.2 0.0 copy-start
  7.2 0.0 all-gather.3.cloned.1.call-start
  7.2 0.7 all-gather.3.cloned.1.call-update
  7.9 0.0 reduce-scatter.2.cloned.1.call-start
  8.0 105.1 %all-gather.3.cloned.1.call-done = bf16[2048,1024]{1,0:T(8,128)(2,1)} async-done(((bf16[64,1024]{1,0:T(8,128)(2,1)}), bf16[2048,1024]{1,0:T(8,128)(2,1)}) %all-gather.3.cloned.1.call-update) | async-done | bytes 4194320 | tf_op jit(solution)/shard_map/all_gather | solution.py:15
  113.0 0.0 copy-done
  113.0 6.5 fusion.8
  119.5 0.0 copy-start.2
  119.5 0.0 copy-start.3
  119.5 0.0 reduce-scatter.2.cloned.1.call-update
  119.5 0.0 all-gather.5.cloned.1.call-start
  119.6 98.7 %reduce-scatter.2.cloned.1.call-done = f32[128,512]{1,0:T(8,128)} async-done(((f32[2048,512]{1,0:T(8,128)}), f32[128,512]{1,0:T(8,128)}) %reduce-scatter.2.cloned.1.call-update) | async-done | bytes 262160 | tf_op jit(solution)/shard_map/reduce_scatter | solution.py:17
  218.3 0.0 copy-done.2
  218.3 1.1 multiply_reduce_fusion
  219.4 88.8 %psum.21 = f32[128,1]{0,1:T(1,128)S(1)} all-reduce(f32[128,1]{0,1:T(1,128)S(1)} %bitcast.6), channel_id=1, replica_groups=mesh['row'=16,'col'=32] {'col'}, use_global_device_ids=true, to_apply=%region_2.0 | all-reduce | flops 128 | bytes 1024 | tf_op jit(solution)/shard_map/psum | solution.py:20
  308.2 0.0 copy-done.3
  308.2 1.7 multiply_convert_fusion
  309.9 0.0 all-gather.5.cloned.1.call-update
  309.9 0.0 all-reduce.3.cloned.1.call-start
  310.0 77.0 %all-gather.5.cloned.1.call-done = bf16[2048,512]{1,0:T(8,128)(2,1)} async-done(((bf16[128,512]{1,0:T(8,128)(2,1)}), bf16[2048,512]{1,0:T(8,128)(2,1)}) %all-gather.5.cloned.1.call-update) | async-done | bytes 2097168 | tf_op jit(solution)/shard_map/all_gather | solution.py:22
  387.0 3.9 broadcast_select_fusion.1
  390.9 0.0 copy-start.1
  390.9 0.0 all-reduce.3.cloned.1.call-update
  391.0 385.4 %all-reduce.3.cloned.1.call-done = (bf16[2048,512]{1,0:T(8,128)(2,1)}, bf16[2048,512]{1,0:T(8,128)(2,1)}) async-done(((bf16[2048,512]{1,0:T(8,128)(2,1)}, bf16[2048,512]{1,0:T(8,128)(2,1)}), (bf16[2048,512]{1,0:T(8,128)(2,1)}, bf16[2048,512]{1,0:T(8,128)(2,1)})) %all-reduce.3.cloned.1.call-update) | async-done | bytes 4194320 | tf_op jit(solution)/shard_map/psum | solution.py:11
  776.3 0.0 copy-done.1
  776.3 5.9 multiply_select_fusion
  (3 shorter events, 0.0 us)
Async XLA Ops:
  7.2 105.9 %copy-start = (bf16[1024,512]{1,0:T(8,128)(2,1)S(1)}, bf16[1024,512]{1,0:T(8,128)(2,1)}, u32[]{:S(2)}) copy-start(bf16[1024,512]{1,0:T(8,128)(2,1)} %param.5) | copy-start | bytes 3145732
  7.2 105.8 %all-gather.3.cloned.1.call-start = ((), (), s32[]{:S(2)}) async-start(), calls=%async_computation.1 | async-start | bytes 4325376 | tf_op jit(solution)/shard_map/all_gather | solution.py:15
  7.9 210.4 %reduce-scatter.2.cloned.1.call-start = ((), (), s32[]{:S(2)}) async-start(), calls=%async_computation.2 | async-start | bytes 4456448 | tf_op jit(solution)/shard_map/reduce_scatter | solution.py:17
  119.5 98.8 %copy-start.2 = (bf16[128,512]{1,0:T(8,128)(2,1)S(1)}, bf16[128,512]{1,0:T(8,128)(2,1)}, u32[]{:S(2)}) copy-start(bf16[128,512]{1,0:T(8,128)(2,1)} %param.6) | copy-start | bytes 393220
  119.5 188.7 %copy-start.3 = (f32[512]{0:T(512)S(1)}, f32[512]{0:T(512)}, u32[]{:S(2)}) copy-start(f32[512]{0:T(512)} %param.7) | copy-start | bytes 6148
  119.5 267.5 %all-gather.5.cloned.1.call-start = ((), (), s32[]{:S(2)}) async-start(), calls=%async_computation.3 | async-start | bytes 2228224 | tf_op jit(solution)/shard_map/all_gather | solution.py:22
  309.9 466.4 %all-reduce.3.cloned.1.call-start = ((), (), s32[]{:S(2)}) async-start(), calls=%async_computation.4 | async-start | bytes 8388608 | tf_op jit(solution)/shard_map/psum | solution.py:11
  390.9 385.4 %copy-start.1 = (bf16[2048,512]{1,0:T(8,128)(2,1)S(1)}, bf16[2048,512]{1,0:T(8,128)(2,1)}, u32[]{:S(2)}) copy-start(bf16[2048,512]{1,0:T(8,128)(2,1)} %all-gather.5.cloned.1.call-done) | copy-start | bytes 6291460
Sparse Core Ops, SparseCore 0:
  11.1 101.8 all-gather.2
  119.6 98.6 reduce-scatter.1
  310.0 76.9 all-gather.4
  391.1 385.2 all-reduce.2
where the time goes:
time: 797 us; the launch traced here: 789 us
  waiting for transfers between devices  667 us (84%)
  blocking collectives  88.8 us (11%)
  between operations  13.8 us (2%)
  matrix products  12.4 us (2%)
    psum x1, waiting for transfers between devices, spread(): return lax.psum(block, axis)  385 us
    all_gather x1, waiting for transfers between devices, local(): gathered = lax.all_gather(attn, 'col', axis=0, tiled=True)  105 us
    reduce_scatter x1, waiting for transfers between devices, local(): lax.psum_scatter(partial_sums, 'row', scatter_dimension=0, tiled=True)  98.7 us
    psum x1, blocking collectives, local(): squares = lax.psum(jnp.sum(summed * summed, axis=1, keepdims=True), 'col')  88.8 us
    all_gather x1, waiting for transfers between devices, local(): col_data = lax.all_gather(normed, 'row', axis=0, tiled=True)  77 us
  transfers between devices with their start and end apart: 4, of which 4 were waited for; matrix products, arithmetic and copies ran while one was open for 0% of the time, Pallas kernels for 0%

commit v1 on v0

v1 whole, which is shorter than its diff:
```python
import jax
import jax.numpy as jnp
from jax import lax
from jax.experimental import pallas as pl
from jax.experimental.pallas import tpu as pltpu
from jax.sharding import PartitionSpec as P

D = 16384
TOKENS = 2048
EPS = 1e-05
MESH = pl.DeviceIdType.MESH
F32 = jnp.float32
BF16 = jnp.bfloat16
ORDER = (0, 1, 3, 2)


def device(x, zl, y, zh, k):
    return (x * 4 + zl, (y * 4 + zh) * 2 + k)


def kernel(
    attn, w_out, resid, gain,
    stream, gram,
    A, W, XS, XR, ACC, ZS, ZR, RB, G, SUM, S2, SR, SQS, SQ, N, M, C, CS, R,
    loc, ks, kr, zs, zr, ys, yr, xs, xr, ls, lr, qs, qr, ms, mr, hs, hr,
    vs, vr, cs, cr, es, er,
):
    row, col = lax.axis_index("row"), lax.axis_index("col")
    x, zl = row // 4, row % 4
    y, zh, k = col // 8, (col // 2) % 4, col % 2
    other = 1 - k

    def at(dx=0, dl=0, dy=0, dh=0):
        return device((x + dx) % 4, (zl + dl) % 4, (y + dy) % 4, (zh + dh) % 4, k)

    sibling = device(x, zl, y, zh, other)
    sends = []

    def copy(src, dst, ssem, rsem, to):
        return pltpu.make_async_remote_copy(
            src_ref=src, dst_ref=dst, send_sem=ssem, recv_sem=rsem,
            device_id=to, device_id_type=MESH,
        )

    def send(src, dst, ssem, rsem, to, when=None):
        c = copy(src, dst, ssem, rsem, to)
        if when is None:
            c.start()
        else:
            pl.when(when)(c.start)
        sends.append((c, when))

    def arrived(dst, ssem, rsem, when=None):
        c = copy(dst, dst, ssem, rsem, sibling)
        if when is None:
            c.wait_recv()
        else:
            pl.when(when)(c.wait_recv)

    bar = pltpu.get_barrier_semaphore()

    def greet(dev, when=None):
        def go():
            pl.semaphore_signal(bar, inc=1, device_id=dev, device_id_type=MESH)
        if when is None:
            go()
        else:
            pl.when(when)(go)

    greet(sibling)
    for d in range(1, 4):
        greet(at(dx=d))
        greet(at(dl=d))
    for dy in range(4):
        for dh in range(4):
            if dy or dh:
                greet(at(dy=dy, dh=dh))
    for s in range(4):
        greet(device(s, zl, x, zh, k), jnp.logical_or(x != y, x != s))
        greet(device(x, s, y, zl, k), jnp.logical_or(zl != zh, zl != s))
    pl.semaphore_wait(
        bar, 22 + 8 - (x == y).astype(jnp.int32) - (zl == zh).astype(jnp.int32)
    )

    for d in (1, 3, 2):
        send(attn, A.at[y, zh], zs.at[d], zr.at[d], at(dh=d))
    for d in (1, 3, 2):
        send(attn, A.at[y, zh], ys.at[0, d], yr.at[0, d], at(dy=d))
    own_w = pltpu.make_async_copy(w_out, W.at[k], loc.at[0])
    own_w.start()
    send(w_out, W.at[k], ks.at[0], kr.at[0], sibling)
    off_other = pl.multiple_of(other * 64, 64)
    off_mine = pl.multiple_of(k * 64, 64)
    send(resid.at[pl.ds(off_other, 64)], RB.at[k], ks.at[1], kr.at[1], sibling)
    send(gain, G.at[k], ks.at[2], kr.at[2], sibling)
    A[y, zh] = attn[...]
    RB[k] = resid[pl.ds(off_mine, 64), :]
    G[k] = gain[...]
    own_w.wait()
    arrived(W.at[other], ks.at[0], kr.at[0])

    def project(i, jz):
        zp = (zh + 4 - jz) % 4

        @pl.loop(0, 4)
        def _(jy):
            yp = (y + 4 - jy) % 4

            @pl.when(jy > 0)
            def _():
                arrived(A.at[yp, zp], ys.at[jz, jy], yr.at[jz, jy])

            for h in range(2):
                part = jnp.dot(A[yp, zp], W[h], preferred_element_type=F32)
                XS[yp, zp, :, h * 512:(h + 1) * 512] = part.astype(BF16)

                @pl.when(yp == x)
                def _():
                    ACC[zp, :, h * 512:(h + 1) * 512] = part

            @pl.when(yp != x)
            def _():
                copy(
                    XS.at[yp, zp], XR.at[x, zp], xs.at[jy, jz], xr.at[x, jz],
                    device(yp, zl, y, zh, k),
                ).start()

    def combine(jz):
        zp = (zh + 4 - jz) % 4
        total = ACC[zp]
        for d in range(1, 4):
            src = (x + d) % 4
            arrived(XR.at[src, zp], xs.at[0, 0], xr.at[src, jz])
            total = total + XR[src, zp].astype(F32)

        @pl.when(zp == zl)
        def _():
            SUM[...] = total

        @pl.when(zp != zl)
        def _():
            ZS[zp] = total.astype(BF16)
            copy(
                ZS.at[zp], ZR.at[zl], ls.at[jz], lr.at[zl], device(x, zp, y, zh, k)
            ).start()

    project(0, 0)
    for jz in (1, 3, 2):
        zp = (zh + 4 - jz) % 4
        arrived(A.at[y, zp], zs.at[jz], zr.at[jz])
        for d in (1, 3, 2):
            send(A.at[y, zp], A.at[y, zp], ys.at[jz, d], yr.at[jz, d], at(dy=d))
    project(1, 1)
    combine(0)
    project(2, 3)
    combine(1)
    project(3, 2)
    combine(3)
    combine(2)

    arrived(RB.at[other], ks.at[1], kr.at[1])
    arrived(G.at[other], ks.at[2], kr.at[2])
    for d in range(1, 4):
        src = (zl + d) % 4
        arrived(ZR.at[src], ls.at[0], lr.at[src])
    squares = jnp.zeros((64, 1), F32)
    for h in range(2):
        part = slice(h * 512, (h + 1) * 512)
        total = SUM[:, part]
        for d in range(1, 4):
            total = total + ZR[(zl + d) % 4, :, part].astype(F32)
        total = total + RB[h].astype(F32)
        SUM[:, part] = total
        S2[h] = total.astype(BF16)
        squares = squares + jnp.sum(total * total, axis=1, keepdims=True)
    wide = jnp.concatenate(
        [jnp.broadcast_to(squares, (64, 128)), jnp.zeros((64, 128), F32)], axis=0
    )
    flat = wide.T
    SQS[...] = flat[0:8]
    for dy in range(4):
        for dh in range(4):
            if dy or dh:
                i = dy * 4 + dh
                send(SQS, SQ.at[i], qs.at[i], qr.at[i], at(dy=dy, dh=dh))
    send(S2.at[other], SR, ks.at[3], kr.at[3], sibling)
    stream[pl.ds(off_mine, 64), :] = S2[k]
    total = SQS[...]
    for i in range(1, 16):
        arrived(SQ.at[i], qs.at[i], qr.at[i])
        total = total + SQ[i]
    scale = lax.rsqrt(total / D + EPS)
    scale = jnp.broadcast_to(scale[0:1], (128, 128)).T[0:64, 0:1]
    for h in range(2):
        part = slice(h * 512, (h + 1) * 512)
        normed = SUM[:, part] * G[h] * scale
        N[h] = normed.astype(BF16).reshape(4, 16, 512)

    for q in range(4):
        away = jnp.logical_or(x != y, y != q)
        send(N.at[:, q], M.at[:, x], ms.at[q], mr.at[x], device(y, zl, q, zh, k), away)
    for d in (1, 3, 2):
        send(N, C.at[:, :, zl, x], hs.at[d], hr.at[d], at(dl=d))
    for d in (1, 3, 2):
        send(N, C.at[:, :, zl, x], cs.at[0, d], cr.at[0, d], at(dx=d))

    @pl.when(x == y)
    def _():
        for h in range(2):
            M[h, x] = N[h, y]

    for h in range(2):
        for q in range(4):
            C[h, q, zl, x] = N[h, q]
    for s in range(4):
        arrived(M.at[:, s], ms.at[0], mr.at[s], jnp.logical_or(x != y, x != s))
    for j in range(4):
        away = jnp.logical_or(zl != zh, zh != j)
        send(M, R.at[k, y, zl], vs.at[j], vr.at[zl], device(x, zh, y, j, k), away)

    @pl.when(zl == zh)
    def _():
        R[k, y, zl] = M[...]

    for dl in (1, 3, 2):
        lp = (zl + 4 - dl) % 4
        arrived(C.at[:, :, lp, x], hs.at[dl], hr.at[dl])
        for d in (1, 3, 2):
            piece = C.at[:, :, lp, x]
            send(piece, piece, cs.at[dl, d], cr.at[dl, d], at(dx=d))
    for s in range(4):
        arrived(R.at[k, y, s], vs.at[0], vr.at[s], jnp.logical_or(zl != zh, zl != s))
        for d in (1, 3, 2):
            piece = R.at[k, y, s]
            send(piece, piece, es.at[s, d], er.at[s, d], at(dy=d))
    send(R.at[k, y], R.at[k, y], ks.at[4], kr.at[4], sibling)
    for dl in range(4):
        for dx in range(1, 4):
            piece = C.at[:, :, (zl + 4 - dl) % 4, (x + 4 - dx) % 4]
            arrived(piece, cs.at[dl, dx], cr.at[dl, dx])
    send(C.at[other], CS, ks.at[8], kr.at[8], sibling)
    arrived(SR, ks.at[3], kr.at[3])
    stream[pl.ds(off_other, 64), :] = SR[...]
    arrived(CS, ks.at[8], kr.at[8])

    def accumulate(q, first, last):
        @pl.loop(0, 2)
        def _(h):
            for half in range(2):
                lanes = slice(half * 256, (half + 1) * 256)
                tile = None
                for lane, rhs in ((k, C.at[k]), (other, CS)):
                    left = R[lane, q, :, h, :, :, lanes].reshape(256, 256)
                    right = rhs[q].reshape(256, 512)
                    term = lax.dot_general(
                        left, right, (((0,), (0,)), ((), ())),
                        preferred_element_type=F32,
                    )
                    tile = term if tile is None else tile + term
                start = pl.multiple_of(h * 512 + half * 256, 256)
                rows = pl.ds(start, 256)
                if not first:
                    tile = tile + gram[rows, :]
                if last:
                    tile = tile * (2.0 / TOKENS)
                    rid = row * 1024 + start + lax.broadcasted_iota(
                        jnp.int32, (256, 512), 0
                    )
                    cid = col * 512 + lax.broadcasted_iota(jnp.int32, (256, 512), 1)
                    tile = jnp.where(cid >= rid, tile, 0.0)
                gram[rows, :] = tile

    for jy in range(4):
        q = (y + 4 - jy) % 4
        if jy:
            for s in range(4):
                arrived(R.at[k, q, s], es.at[s, jy], er.at[s, jy])
            send(R.at[k, q], R.at[k, q], ks.at[4 + jy], kr.at[4 + jy], sibling)
        arrived(R.at[other, q], ks.at[4 + jy], kr.at[4 + jy])
        accumulate(q, jy == 0, jy == 3)

    for c, when in sends:
        if when is None:
            c.wait_send()
        else:
            pl.when(when)(c.wait_send)
    for jz in range(4):
        zp = (zh + 4 - jz) % 4
        for jy in range(4):
            yp = (y + 4 - jy) % 4
            c = copy(
                XS.at[yp, zp], XR.at[x, zp], xs.at[jy, jz], xr.at[x, jz],
                device(yp, zl, y, zh, k),
            )
            pl.when(yp != x)(c.wait_send)
        c = copy(ZS.at[zp], ZR.at[zl], ls.at[jz], lr.at[zl], device(x, zp, y, zh, k))
        pl.when(zp != zl)(c.wait_send)


def local(attn, w_out, resid, gain):
    dma = pltpu.SemaphoreType.DMA
    vmem = pltpu.VMEM
    whole = pl.BlockSpec(memory_space=pltpu.VMEM)
    return pl.pallas_call(
        kernel,
        out_shape=(
            jax.ShapeDtypeStruct((128, 512), BF16),
            jax.ShapeDtypeStruct((1024, 512), F32),
        ),
        in_specs=[whole, pl.BlockSpec(memory_space=pl.ANY), whole, whole],
        out_specs=(whole, whole),
        scratch_shapes=[
            vmem((4, 4, 64, 1024), BF16),
            vmem((2, 1024, 512), BF16),
            vmem((4, 4, 64, 1024), BF16),
            vmem((4, 4, 64, 1024), BF16),
            vmem((4, 64, 1024), F32),
            vmem((4, 64, 1024), BF16),
            vmem((4, 64, 1024), BF16),
            vmem((2, 64, 512), BF16),
            vmem((2, 1, 512), F32),
            vmem((64, 1024), F32),
            vmem((2, 64, 512), BF16),
            vmem((64, 512), BF16),
            vmem((8, 128), F32),
            vmem((16, 8, 128), F32),
            vmem((2, 4, 16, 512), BF16),
            vmem((2, 4, 16, 512), BF16),
            vmem((2, 4, 4, 4, 16, 512), BF16),
            vmem((4, 4, 4, 16, 512), BF16),
            vmem((2, 4, 4, 2, 4, 16, 512), BF16),
            dma((1,)), dma((9,)), dma((9,)), dma((4,)), dma((4,)),
            dma((4, 4)), dma((4, 4)), dma((4, 4)), dma((4, 4)),
            dma((4,)), dma((4,)), dma((16,)), dma((16,)), dma((4,)), dma((4,)),
            dma((4,)), dma((4,)), dma((4,)), dma((4,)), dma((4, 4)), dma((4, 4)),
            dma((4, 4)), dma((4, 4)),
        ],
        compiler_params=pltpu.CompilerParams(
            collective_id=0, has_side_effects=True, vmem_limit_bytes=48 << 20
        ),
        cost_estimate=pl.CostEstimate(
            flops=4 * 2048 * 1024 * 512, bytes_accessed=16 << 20, transcendentals=128
        ),
    )(attn, w_out, resid, gain.reshape(1, 512))


def solution(mesh):
    placed = (P("col", "row"), P("row", "col"), P("row", "col"), P("col"))
    return jax.shard_map(
        local,
        mesh=mesh,
        in_specs=placed,
        out_specs=(P("row", "col"), P("row", "col")),
        check_vma=False,
    )
```

time: 797 us -> 155 us (0.19)
  the two profiles are of different devices: /device:TPU:1 before, /device:TPU:97 now
where the time goes in v1:
time: 155 us
  Pallas kernels  149 us (96%)
  local copies, waits for them, and re-layouts  5.68 us (4%)
    pallas_call x1, Pallas kernels, local(): pl.pallas_call(kernel, out_shape=(jax.ShapeDtypeStruct((128, 512), BF16),...  149 us
    unnamed x10, local copies, waits for them, and re-layouts  5.68 us

profile of v1, /device:TPU:97, one launch (start us, length us, event | category | flops | bytes accessed | tf_op | source)
XLA Modules:
  0.0 155.1 jit_solution(12093589040152309382)
XLA Ops:
  0.6 0.0 copy-start
  0.6 1.2 copy-done
  1.9 0.0 copy-start.1
  1.9 0.9 copy-done.1
  2.8 0.0 copy-start.2
  2.8 0.9 copy-done.2
  3.7 0.0 copy-start.3
  3.7 0.7 copy-done.3
  4.3 148.7 %shard_map.59 = (bf16[128,512]{1,0:T(8,128)(2,1)S(1)}, f32[1024,512]{1,0:T(8,128)S(1)}) custom-call(bf16[64,1024]{1,0:T(8,128)(2,1)S(1)} %copy-done.1, bf16[1024,512]{1,0:T(8,128)(2,1)S(1)} %copy-done, bf16[128,512]{1,0:T(8,128)(2,1)S(1)} %copy-done.2, f32[1,512]{1,0:T(1,128)S(1)} %bitcast.1), custom_call_target="tpu_custom_call" | custom-call | flops 4294967296 | bytes 16777216 | tf_op jit(solution)/shard_map/pallas_call | solution.py:304
  153.1 0.7 copy.8
  153.8 1.3 copy.9
Async XLA Ops:
  0.6 1.2 copy-start
  1.9 0.9 copy-start.1
  2.8 0.9 copy-start.2
  3.7 0.7 copy-start.3

commit v2 on v0

v2 whole, which is shorter than its diff:
```python
import jax
import jax.numpy as jnp
from jax import lax
from jax.experimental import pallas as pl
from jax.experimental.pallas import tpu as pltpu
from jax.sharding import PartitionSpec as P

D = 16384
TOKENS = 2048
EPS = 1e-05
MESH = pl.DeviceIdType.MESH
F32 = jnp.float32
BF16 = jnp.bfloat16
PARTS = 4
T = 64 // PARTS
AHEAD = 2
STEPS = (
    ("attention_z", 36, 5), ("attention_y", 40, 5), ("project", 47, 6),
    ("combine", 55, 6.5), ("squares", 61, 6.5), ("norm", 66, 6.5),
    ("multicast", 70, 7), ("rows_z", 75, 7), ("rows_y", 80, 7), ("rows_core", 88, 7),
    ("gram", 91, 7),
)


def device(x, zl, y, zh, k):
    return (x * 4 + zl, (y * 4 + zh) * 2 + k)


def kernel(
    attn, w_out, resid, gain,
    stream, gram,
    A, W, XS, XR, ACC, ZS, ZR, RB, G, SUM, S2, SR, SQS, SQ, N, M, C, CS, R,
    loc, ks, kr, zs, zr, ys, yr, xs, xr, ls, lr, qs, qr, ms, mr, hs, hr,
    vs, vr, cs, cr, es, er, fs, fr, gs, gr, ts,
):
    row, col = lax.axis_index("row"), lax.axis_index("col")
    x, zl = row // 4, row % 4
    y, zh, k = col // 8, (col // 2) % 4, col % 2
    other = 1 - k

    def at(dx=0, dl=0, dy=0, dh=0):
        return device((x + dx) % 4, (zl + dl) % 4, (y + dy) % 4, (zh + dh) % 4, k)

    sibling = device(x, zl, y, zh, other)
    sends = []

    def copy(src, dst, ssem, rsem, to):
        return pltpu.make_async_remote_copy(
            src_ref=src, dst_ref=dst, send_sem=ssem, recv_sem=rsem,
            device_id=to, device_id_type=MESH,
        )

    def send(src, dst, ssem, rsem, to, when=None):
        c = copy(src, dst, ssem, rsem, to)
        if when is None:
            c.start()
        else:
            pl.when(when)(c.start)
        sends.append((c, when))

    def arrived(dst, ssem, rsem, when=None):
        c = copy(dst, dst, ssem, rsem, sibling)
        if when is None:
            c.wait_recv()
        else:
            pl.when(when)(c.wait_recv)

    off_other = pl.multiple_of(other * 64, 64)
    off_mine = pl.multiple_of(k * 64, 64)
    own = [
        pltpu.make_async_copy(w_out, W.at[k], loc.at[0]),
        pltpu.make_async_copy(resid.at[pl.ds(off_mine, 64)], RB.at[k], loc.at[1]),
        pltpu.make_async_copy(gain, G.at[k], loc.at[2]),
    ] + [
        pltpu.make_async_copy(attn.at[pl.ds(c * T, T)], A.at[c, y, zh], loc.at[3 + c])
        for c in range(PARTS)
    ]
    for c in own:
        c.start()

    bar = pltpu.get_barrier_semaphore()

    def greet(dev, when=None):
        def go():
            pl.semaphore_signal(bar, inc=1, device_id=dev, device_id_type=MESH)
        if when is None:
            go()
        else:
            pl.when(when)(go)

    greet(sibling)
    for d in range(1, 4):
        greet(at(dx=d))
        greet(at(dl=d))
    for dy in range(4):
        for dh in range(4):
            if dy or dh:
                greet(at(dy=dy, dh=dh))
    for s in range(4):
        greet(device(s, zl, x, zh, k), jnp.logical_or(x != y, x != s))
        greet(device(x, s, y, zl, k), jnp.logical_or(zl != zh, zl != s))
    pl.semaphore_wait(
        bar, 22 + 8 - (x == y).astype(jnp.int32) - (zl == zh).astype(jnp.int32)
    )

    def attention_out(c):
        for d in (1, 3):
            send(
                attn.at[pl.ds(c * T, T)], A.at[c, y, zh], zs.at[c, d], zr.at[c, d],
                at(dh=d),
            )

    for c in range(AHEAD):
        attention_out(c)
    send(w_out, W.at[k], ks.at[0], kr.at[0], sibling)
    send(resid.at[pl.ds(off_other, 64)], RB.at[k], ks.at[1], kr.at[1], sibling)
    send(gain, G.at[k], ks.at[2], kr.at[2], sibling)
    for c in own:
        c.wait()
    arrived(W.at[other], ks.at[0], kr.at[0])
    arrived(RB.at[other], ks.at[1], kr.at[1])
    arrived(G.at[other], ks.at[2], kr.at[2])

    def to_x(c, yp):
        return copy(
            XS.at[c, yp], XR.at[c, x], xs.at[c, yp], xr.at[c, x],
            device(yp, zl, y, zh, k),
        )

    def to_zl(c, zp):
        return copy(
            ZS.at[c, zp], ZR.at[c, zl], ls.at[c, zp], lr.at[c, zl],
            device(x, zp, y, zh, k),
        )

    def project_block(c, yp):
        left = A[c, yp].reshape(4 * T, 1024)
        for h in range(2):
            lanes = slice(h * 512, (h + 1) * 512)
            part = jnp.dot(left, W[h], preferred_element_type=F32).reshape(4, T, 512)

            @pl.when(yp == x)
            def _():
                ACC[c, :, :, lanes] = part

            @pl.when(yp != x)
            def _():
                XS[c, yp, :, :, lanes] = part.astype(BF16)

        pl.when(yp != x)(lambda: to_x(c, yp).start())

    def attention_z(c):
        d = 1 if c % 2 == 0 else 3
        piece = A.at[c, y, (zh + 4 - d) % 4]
        arrived(piece, zs.at[c, d], zr.at[c, d])
        send(piece, piece, zs.at[c, 2], zr.at[c, 2], at(dh=d))
        if c + AHEAD < PARTS:
            attention_out(c + AHEAD)

    def attention_y(c):
        for d in ((3, 2) if c % 2 == 0 else (1, 2)):
            arrived(A.at[c, y, (zh + 4 - d) % 4], zs.at[c, d], zr.at[c, d])
        for d in (1, 3, 2):
            send(A.at[c, y], A.at[c, y], ys.at[c, d], yr.at[c, d], at(dy=d))
        project_block(c, y)

    def project(c):
        @pl.loop(1, 4)
        def _(d):
            yp = (y + 4 - d) % 4
            arrived(A.at[c, yp], ys.at[c, d], yr.at[c, d])
            project_block(c, yp)

    def combine(c):
        total = ACC[c]
        for d in range(1, 4):
            src = (x + d) % 4
            arrived(XR.at[c, src], xs.at[c, 0], xr.at[c, src])
            total = total + XR[c, src].astype(F32)
        ACC[c] = total
        ZS[c] = total.astype(BF16)
        for d in (1, 3, 2):
            to_zl(c, (zl + d) % 4).start()

    def squares(c):
        rows = slice(c * T, (c + 1) * T)
        for d in range(1, 4):
            src = (zl + d) % 4
            arrived(ZR.at[c, src], ls.at[c, 0], lr.at[c, src])
        summed_squares = jnp.zeros((T, 1), F32)
        for h in range(2):
            lanes = slice(h * 512, (h + 1) * 512)
            total = ACC[c, zl, :, lanes]
            for d in range(1, 4):
                total = total + ZR[c, (zl + d) % 4, :, lanes].astype(F32)
            total = total + RB[h, rows, :].astype(F32)
            SUM[c, :, lanes] = total
            S2[h, rows, :] = total.astype(BF16)
            summed_squares = summed_squares + jnp.sum(total * total, axis=1, keepdims=True)
        wide = jnp.concatenate(
            [
                jnp.broadcast_to(summed_squares, (T, 128)),
                jnp.zeros((128 - T, 128), F32),
            ],
            axis=0,
        )
        SQS[c] = wide.T[0:1]
        for dh in (2, 1, 3, 0):
            for dy in (2, 1, 3, 0):
                if dy or dh:
                    i = dy * 4 + dh
                    send(
                        SQS.at[c], SQ.at[c, i], qs.at[c, i], qr.at[c, i],
                        at(dy=dy, dh=dh),
                    )
        if c == PARTS - 1:
            send(S2.at[other], SR, ks.at[3], kr.at[3], sibling)

    def norm(c):
        total = SQS[c]
        for i in range(1, 16):
            arrived(SQ.at[c, i], qs.at[c, i], qr.at[c, i])
            total = total + SQ[c, i]
        scale = lax.rsqrt(total / D + EPS)
        scale = jnp.broadcast_to(scale, (128, 128)).T[0:T, 0:1]
        for f in range(4):
            lanes = slice(f * 256, (f + 1) * 256)
            g = G[f // 2, :, (f % 2) * 256:(f % 2) * 256 + 256]
            normed = (SUM[c, :, lanes] * g * scale).astype(BF16)
            N[c, f] = normed
            C[c, zl, x, f] = normed

        @pl.when(x == y)
        def _():
            M[c, x] = N[c, y]

        for q in range(4):
            away = jnp.logical_or(x != y, y != q)
            send(
                N.at[c, q], M.at[c, x], ms.at[c, q], mr.at[c, x],
                device(y, zl, q, zh, k), away,
            )
        for d in (1, 3, 2):
            send(N.at[c], C.at[c, zl, x], hs.at[c, d], hr.at[c, d], at(dl=d))

    def multicast(c):
        for s in range(4):
            arrived(
                M.at[c, s], ms.at[c, 0], mr.at[c, s], jnp.logical_or(x != y, x != s)
            )
        up = (zh + (zl > zh).astype(jnp.int32)) % 4
        for i, (j, away) in enumerate(((up, zl != zh), ((up + 3) % 4, None))):
            send(
                M.at[c], R.at[k, c, y, zl], vs.at[c, i], vr.at[c, zl],
                device(x, zh, y, j, k), away,
            )

        @pl.when(zl == zh)
        def _():
            R[k, c, y, zl] = M[c]

        for d in (1, 3, 2):
            arrived(C.at[c, (zl + 4 - d) % 4, x], hs.at[c, d], hr.at[c, d])
        for d in (1, 3, 2):
            piece = C.at[c, :, x]
            send(piece, piece, cs.at[c, d], cr.at[c, d], at(dx=d))

    def direct(s):
        up = (zl + (zl < s).astype(jnp.int32)) % 4
        return zh == up, zh == (up + 3) % 4

    def rows_z(c):
        for s in range(4):
            above, below = direct(s)
            piece = R.at[k, c, y, s]
            first = jnp.logical_or(above, below)
            here = jnp.logical_and(zl == zh, zl == s)
            arrived(
                piece, vs.at[c, 0], vr.at[c, s],
                jnp.logical_and(first, jnp.logical_not(here)),
            )
            to = jnp.where(above, 1, 3)
            send(piece, piece, ts.at[c, s], vr.at[c, s], at(dh=to), first)

    def rows_y(c):
        piece = R.at[k, c, y]
        for s in range(4):
            above, below = direct(s)
            arrived(
                R.at[k, c, y, s], vs.at[c, 0], vr.at[c, s],
                jnp.logical_not(jnp.logical_or(above, below)),
            )
        for d in (1, 3, 2):
            send(piece, piece, es.at[c, d], er.at[c, d], at(dy=d))
        send(piece, piece, fs.at[c, 0], fr.at[c, 0], sibling)

    def rows_core(c):
        for d in (1, 3, 2):
            arrived(C.at[c, :, (x + 4 - d) % 4], cs.at[c, d], cr.at[c, d])
        send(C.at[c, :, :, pl.ds(2 * other, 2)], CS.at[c], gs.at[c], gr.at[c], sibling)
        for d in (1, 3, 2):
            piece = R.at[k, c, (y + 4 - d) % 4]
            arrived(piece, es.at[c, d], er.at[c, d])
            send(piece, piece, fs.at[c, d], fr.at[c, d], sibling)

    def gram_part(c):
        arrived(CS.at[c], gs.at[c], gr.at[c])
        for d in range(4):
            arrived(R.at[other, c, (y + 4 - d) % 4], fs.at[c, d], fr.at[c, d])

        @pl.loop(0, 4)
        def _(f):
            start = pl.multiple_of(f * 256, 256)
            rows = pl.ds(start, 256)
            for half in range(2):
                lanes = slice(half * 256, (half + 1) * 256)
                tile = None if c == 0 else gram[rows, lanes]
                for lane in range(2):
                    left = R[k if lane == 0 else other, c, f].reshape(16 * T, 256)
                    right = C[c, :, :, 2 * k + half] if lane == 0 else CS[c, :, :, half]
                    term = lax.dot_general(
                        left, right.reshape(16 * T, 256), (((0,), (0,)), ((), ())),
                        preferred_element_type=F32,
                    )
                    tile = term if tile is None else tile + term
                if c == PARTS - 1:
                    tile = tile * (2.0 / TOKENS)
                    rid = row * 1024 + start + lax.broadcasted_iota(
                        jnp.int32, (256, 256), 0
                    )
                    cid = col * 512 + half * 256 + lax.broadcasted_iota(
                        jnp.int32, (256, 256), 1
                    )
                    tile = jnp.where(cid >= rid, tile, 0.0)
                gram[rows, lanes] = tile

    steps = {
        "attention_z": attention_z, "attention_y": attention_y, "project": project, "combine": combine,
        "squares": squares, "norm": norm, "multicast": multicast, "rows_z": rows_z,
        "rows_y": rows_y, "rows_core": rows_core, "gram": gram_part,
    }
    order = sorted(
        (start + pitch * c, c, name) for name, start, pitch in STEPS for c in range(PARTS)
    )
    for _, c, name in order:
        steps[name](c)

    arrived(SR, ks.at[3], kr.at[3])
    stream[pl.ds(off_mine, 64), :] = S2[k]
    stream[pl.ds(off_other, 64), :] = SR[...]
    for c, when in sends:
        if when is None:
            c.wait_send()
        else:
            pl.when(when)(c.wait_send)
    for c in range(PARTS):
        for d in range(4):
            yp = (y + 4 - d) % 4
            pl.when(yp != x)(to_x(c, yp).wait_send)
            if d:
                to_zl(c, (zl + d) % 4).wait_send()


def local(attn, w_out, resid, gain):
    dma = pltpu.SemaphoreType.DMA
    vmem = pltpu.VMEM
    whole = pl.BlockSpec(memory_space=pltpu.VMEM)
    anywhere = pl.BlockSpec(memory_space=pl.ANY)
    parts = dma((PARTS, 4))
    return pl.pallas_call(
        kernel,
        out_shape=(
            jax.ShapeDtypeStruct((128, 512), BF16),
            jax.ShapeDtypeStruct((1024, 512), F32),
        ),
        in_specs=[anywhere] * 4,
        out_specs=(whole, whole),
        scratch_shapes=[
            vmem((PARTS, 4, 4, T, 1024), BF16),
            vmem((2, 1024, 512), BF16),
            vmem((PARTS, 4, 4, T, 1024), BF16),
            vmem((PARTS, 4, 4, T, 1024), BF16),
            vmem((PARTS, 4, T, 1024), F32),
            vmem((PARTS, 4, T, 1024), BF16),
            vmem((PARTS, 4, T, 1024), BF16),
            vmem((2, 64, 512), BF16),
            vmem((2, 1, 512), F32),
            vmem((PARTS, T, 1024), F32),
            vmem((2, 64, 512), BF16),
            vmem((64, 512), BF16),
            vmem((PARTS, 1, 128), F32),
            vmem((PARTS, 16, 1, 128), F32),
            vmem((PARTS, 4, T, 256), BF16),
            vmem((PARTS, 4, T, 256), BF16),
            vmem((PARTS, 4, 4, 4, T, 256), BF16),
            vmem((PARTS, 4, 4, 2, T, 256), BF16),
            vmem((2, PARTS, 4, 4, 4, T, 256), BF16),
            dma((3 + PARTS,)), dma((4,)), dma((4,)),
            parts, parts, parts, parts, parts, parts, parts, parts,
            dma((PARTS, 16)), dma((PARTS, 16)),
            parts, parts, parts, parts, parts, parts, parts, parts, parts, parts,
            parts, parts, dma((PARTS,)), dma((PARTS,)), parts,
        ],
        compiler_params=pltpu.CompilerParams(
            collective_id=0, has_side_effects=True, vmem_limit_bytes=60 << 20
        ),
        cost_estimate=pl.CostEstimate(
            flops=4 * 2048 * 1024 * 512, bytes_accessed=16 << 20, transcendentals=128
        ),
    )(attn, w_out, resid, gain.reshape(1, 512))


def solution(mesh):
    placed = (P("col", "row"), P("row", "col"), P("row", "col"), P("col"))
    return jax.shard_map(
        local,
        mesh=mesh,
        in_specs=placed,
        out_specs=(P("row", "col"), P("row", "col")),
        check_vma=False,
    )
```

time: 797 us -> 135 us (0.17)
  the two profiles are of different devices: /device:TPU:1 before, /device:TPU:35 now
where the time goes in v2:
time: 135 us
  Pallas kernels  130 us (96%)
  local copies, waits for them, and re-layouts  4.65 us (3%)
    pallas_call x1, Pallas kernels, local(): pl.pallas_call(kernel, out_shape=(jax.ShapeDtypeStruct((128, 512), BF16),...  130 us
    unnamed x2, local copies, waits for them, and re-layouts  4.65 us

profile of v2, /device:TPU:35, one launch (start us, length us, event | category | flops | bytes accessed | tf_op | source)
XLA Modules:
  0.0 134.9 jit_solution(13563854086371394807)
XLA Ops:
  0.6 129.6 %shard_map.59 = (bf16[128,512]{1,0:T(8,128)(2,1)}, f32[1024,512]{1,0:T(8,128)}) custom-call(bf16[64,1024]{1,0:T(8,128)(2,1)} %attn.1, bf16[1024,512]{1,0:T(8,128)(2,1)} %w_out.1, bf16[128,512]{1,0:T(8,128)(2,1)} %resid.1, f32[1,512]{1,0:T(1,128)} %bitcast.1), custom_call_target="tpu_custom_call" | custom-call | flops 4294967296 | bytes 16777216 | tf_op jit(solution)/shard_map/pallas_call | solution.py:370
  130.2 1.6 %copy.8 = bf16[128,512]{1,0:T(8,128)(2,1)} copy(bf16[128,512]{1,0:T(8,128)(2,1)} %get-tuple-element.4) | data formatting | bytes 262144
  131.8 3.1 %copy.9 = f32[1024,512]{1,0:T(8,128)} copy(f32[1024,512]{1,0:T(8,128)} %get-tuple-element.5) | data formatting | bytes 4194304

commit v3 on v2

--- a/solution.py
+++ b/solution.py
@@ -15,10 +15,9 @@
 T = 64 // PARTS
 AHEAD = 2
 STEPS = (
-    ("attention_z", 36, 5), ("attention_y", 40, 5), ("project", 47, 6),
-    ("combine", 55, 6.5), ("squares", 61, 6.5), ("norm", 66, 6.5),
-    ("multicast", 70, 7), ("rows_z", 75, 7), ("rows_y", 80, 7), ("rows_core", 88, 7),
-    ("gram", 91, 7),
+    ("attention_z", 39, 4), ("attention_y", 43, 4.5), ("project", 51, 5),
+    ("combine", 60, 5), ("squares", 65, 5), ("norm", 72, 5), ("rows_z", 77, 5),
+    ("rows_y", 82, 5), ("columns_x", 83, 5), ("rows_core", 90, 6), ("gram", 93, 6),
 )
 
 
@@ -29,9 +28,9 @@
 def kernel(
     attn, w_out, resid, gain,
     stream, gram,
-    A, W, XS, XR, ACC, ZS, ZR, RB, G, SUM, S2, SR, SQS, SQ, N, M, C, CS, R,
-    loc, ks, kr, zs, zr, ys, yr, xs, xr, ls, lr, qs, qr, ms, mr, hs, hr,
-    vs, vr, cs, cr, es, er, fs, fr, gs, gr, ts,
+    A, W, XS, XR, ACC, ZS, ZR, RB, G, SUM, S2, SR, SQS, SQ, N, C, CS, R,
+    loc, ks, kr, zs, zr, ys, yr, xs, xr, ls, lr, qs, qr, hs, hr,
+    vs, vr, cs, cr, es, er, fs, fr, gs, gr, us, ur,
 ):
     row, col = lax.axis_index("row"), lax.axis_index("col")
     x, zl = row // 4, row % 4
@@ -88,20 +87,23 @@
         else:
             pl.when(when)(go)
 
+    for dh in (2, 1, 3, 0):
+        for dy in (2, 1, 3, 0):
+            if dy or dh:
+                greet(at(dy=dy, dh=dh))
+    diagonal = jnp.logical_and(x == y, zl == zh)
+    for sz in range(4):
+        for sx in range(4):
+            here = jnp.logical_and(sx == x, sz == zl)
+            greet(
+                device(sx, sz, x, zl, k),
+                jnp.logical_not(jnp.logical_and(diagonal, here)),
+            )
     greet(sibling)
     for d in range(1, 4):
         greet(at(dx=d))
         greet(at(dl=d))
-    for dy in range(4):
-        for dh in range(4):
-            if dy or dh:
-                greet(at(dy=dy, dh=dh))
-    for s in range(4):
-        greet(device(s, zl, x, zh, k), jnp.logical_or(x != y, x != s))
-        greet(device(x, s, y, zl, k), jnp.logical_or(zl != zh, zl != s))
-    pl.semaphore_wait(
-        bar, 22 + 8 - (x == y).astype(jnp.int32) - (zl == zh).astype(jnp.int32)
-    )
+    pl.semaphore_wait(bar, 22 + 16 - diagonal.astype(jnp.int32))
 
     def attention_out(c):
         for d in (1, 3):
@@ -230,65 +232,60 @@
             N[c, f] = normed
             C[c, zl, x, f] = normed
 
-        @pl.when(x == y)
+        up = (zh + (zh < zl).astype(jnp.int32)) % 4
+        for i in range(2):
+            j = (up + 3 * i) % 4
+            for q in range(4):
+                away = None
+                if i == 0:
+                    away = jnp.logical_not(jnp.logical_and(diagonal, q == y))
+                send(
+                    N.at[c, q], R.at[k, c, q, zl, x],
+                    vs.at[c, 4 * i + q], vr.at[c, 4 * zl + x],
+                    device(y, zh, q, j, k), away,
+                )
+
+        @pl.when(diagonal)
         def _():
-            M[c, x] = N[c, y]
-
-        for q in range(4):
-            away = jnp.logical_or(x != y, y != q)
-            send(
-                N.at[c, q], M.at[c, x], ms.at[c, q], mr.at[c, x],
-                device(y, zl, q, zh, k), away,
-            )
+            R[k, c, y, zl, x] = N[c, y]
+
         for d in (1, 3, 2):
             send(N.at[c], C.at[c, zl, x], hs.at[c, d], hr.at[c, d], at(dl=d))
 
-    def multicast(c):
-        for s in range(4):
-            arrived(
-                M.at[c, s], ms.at[c, 0], mr.at[c, s], jnp.logical_or(x != y, x != s)
-            )
-        up = (zh + (zl > zh).astype(jnp.int32)) % 4
-        for i, (j, away) in enumerate(((up, zl != zh), ((up + 3) % 4, None))):
-            send(
-                M.at[c], R.at[k, c, y, zl], vs.at[c, i], vr.at[c, zl],
-                device(x, zh, y, j, k), away,
-            )
-
-        @pl.when(zl == zh)
-        def _():
-            R[k, c, y, zl] = M[c]
-
+    def columns_x(c):
         for d in (1, 3, 2):
             arrived(C.at[c, (zl + 4 - d) % 4, x], hs.at[c, d], hr.at[c, d])
         for d in (1, 3, 2):
             piece = C.at[c, :, x]
             send(piece, piece, cs.at[c, d], cr.at[c, d], at(dx=d))
 
-    def direct(s):
-        up = (zl + (zl < s).astype(jnp.int32)) % 4
+    def direct(sz):
+        up = (zl + (zl < sz).astype(jnp.int32)) % 4
         return zh == up, zh == (up + 3) % 4
 
     def rows_z(c):
-        for s in range(4):
-            above, below = direct(s)
-            piece = R.at[k, c, y, s]
-            first = jnp.logical_or(above, below)
-            here = jnp.logical_and(zl == zh, zl == s)
-            arrived(
-                piece, vs.at[c, 0], vr.at[c, s],
-                jnp.logical_and(first, jnp.logical_not(here)),
-            )
-            to = jnp.where(above, 1, 3)
-            send(piece, piece, ts.at[c, s], vr.at[c, s], at(dh=to), first)
+        for sz in range(4):
+            below, above = direct(sz)
+            first = jnp.logical_or(below, above)
+            for sx in range(4):
+                here = jnp.logical_and(sx == x, sz == zl)
+                arrived(
+                    R.at[k, c, y, sz, sx], vs.at[c, 0], vr.at[c, 4 * sz + sx],
+                    jnp.logical_and(
+                        first, jnp.logical_not(jnp.logical_and(diagonal, here))
+                    ),
+                )
+            piece = R.at[k, c, y, sz]
+            to = jnp.where(below, 1, 3)
+            send(piece, piece, us.at[c, sz], ur.at[c, sz], at(dh=to), first)
 
     def rows_y(c):
         piece = R.at[k, c, y]
-        for s in range(4):
-            above, below = direct(s)
+        for sz in range(4):
+            below, above = direct(sz)
             arrived(
-                R.at[k, c, y, s], vs.at[c, 0], vr.at[c, s],
-                jnp.logical_not(jnp.logical_or(above, below)),
+                R.at[k, c, y, sz], us.at[c, sz], ur.at[c, sz],
+                jnp.logical_not(jnp.logical_or(below, above)),
             )
         for d in (1, 3, 2):
             send(piece, piece, es.at[c, d], er.at[c, d], at(dy=d))
@@ -336,7 +333,7 @@
 
     steps = {
         "attention_z": attention_z, "attention_y": attention_y, "project": project, "combine": combine,
-        "squares": squares, "norm": norm, "multicast": multicast, "rows_z": rows_z,
+        "squares": squares, "norm": norm, "columns_x": columns_x, "rows_z": rows_z,
         "rows_y": rows_y, "rows_core": rows_core, "gram": gram_part,
     }
     order = sorted(
@@ -366,7 +363,7 @@
     vmem = pltpu.VMEM
     whole = pl.BlockSpec(memory_space=pltpu.VMEM)
     anywhere = pl.BlockSpec(memory_space=pl.ANY)
-    parts = dma((PARTS, 4))
+    parts, sixteen = dma((PARTS, 4)), dma((PARTS, 16))
     return pl.pallas_call(
         kernel,
         out_shape=(
@@ -391,18 +388,17 @@
             vmem((PARTS, 1, 128), F32),
             vmem((PARTS, 16, 1, 128), F32),
             vmem((PARTS, 4, T, 256), BF16),
-            vmem((PARTS, 4, T, 256), BF16),
             vmem((PARTS, 4, 4, 4, T, 256), BF16),
             vmem((PARTS, 4, 4, 2, T, 256), BF16),
             vmem((2, PARTS, 4, 4, 4, T, 256), BF16),
             dma((3 + PARTS,)), dma((4,)), dma((4,)),
             parts, parts, parts, parts, parts, parts, parts, parts,
-            dma((PARTS, 16)), dma((PARTS, 16)),
-            parts, parts, parts, parts, parts, parts, parts, parts, parts, parts,
-            parts, parts, dma((PARTS,)), dma((PARTS,)), parts,
+            sixteen, sixteen, parts, parts, sixteen, sixteen,
+            parts, parts, parts, parts, parts, parts,
+            dma((PARTS,)), dma((PARTS,)), parts, parts,
         ],
         compiler_params=pltpu.CompilerParams(
-            collective_id=0, has_side_effects=True, vmem_limit_bytes=60 << 20
+            collective_id=0, has_side_effects=True, vmem_limit_bytes=40 << 20
         ),
         cost_estimate=pl.CostEstimate(
             flops=4 * 2048 * 1024 * 512, bytes_accessed=16 << 20, transcendentals=128

time: 135 us -> 130 us (0.963)
  the two profiles are of different devices: /device:TPU:35 before, /device:TPU:1 now
where the time goes in v3:
time: 130 us; the launch traced here: 128 us
  Pallas kernels  122 us (94%)
  local copies, waits for them, and re-layouts  5.68 us (4%)
    pallas_call x1, Pallas kernels, local(): pl.pallas_call(kernel, out_shape=(jax.ShapeDtypeStruct((128, 512), BF16),...  122 us
    unnamed x10, local copies, waits for them, and re-layouts  5.68 us

profile of v3, /device:TPU:1, one launch (start us, length us, event | category | flops | bytes accessed | tf_op | source)
XLA Modules:
  0.0 128.3 jit_solution(9687097153846889509)
XLA Ops:
  0.6 0.0 copy-start
  0.6 1.2 copy-done
  1.9 0.0 copy-start.1
  1.9 0.9 copy-done.1
  2.8 0.0 copy-start.2
  2.8 0.9 copy-done.2
  3.7 0.0 copy-start.3
  3.7 0.7 copy-done.3
  4.3 121.9 %shard_map.59 = (bf16[128,512]{1,0:T(8,128)(2,1)S(1)}, f32[1024,512]{1,0:T(8,128)S(1)}) custom-call(bf16[64,1024]{1,0:T(8,128)(2,1)S(1)} %copy-done.1, bf16[1024,512]{1,0:T(8,128)(2,1)S(1)} %copy-done, bf16[128,512]{1,0:T(8,128)(2,1)S(1)} %copy-done.2, f32[1,512]{1,0:T(1,128)S(1)} %bitcast.1), custom_call_target="tpu_custom_call" | custom-call | flops 4294967296 | bytes 16777216 | tf_op jit(solution)/shard_map/pallas_call | solution.py:367
  126.3 0.7 copy.8
  127.0 1.3 %copy.9 = f32[1024,512]{1,0:T(8,128)} copy(f32[1024,512]{1,0:T(8,128)S(1)} %get-tuple-element.5) | data formatting | bytes 4194304
Async XLA Ops:
  0.6 1.2 copy-start
  1.9 0.9 copy-start.1
  2.8 0.9 copy-start.2
  3.7 0.7 copy-start.3

commit v4 on v3

--- a/solution.py
+++ b/solution.py
@@ -14,6 +14,7 @@
 PARTS = 4
 T = 64 // PARTS
 AHEAD = 2
+DIRECT = 1
 STEPS = (
     ("attention_z", 39, 4), ("attention_y", 43, 4.5), ("project", 51, 5),
     ("combine", 60, 5), ("squares", 65, 5), ("norm", 72, 5), ("rows_z", 77, 5),
@@ -106,7 +107,7 @@
     pl.semaphore_wait(bar, 22 + 16 - diagonal.astype(jnp.int32))
 
     def attention_out(c):
-        for d in (1, 3):
+        for d in (1, 3) if c >= DIRECT else (1, 3, 2):
             send(
                 attn.at[pl.ds(c * T, T)], A.at[c, y, zh], zs.at[c, d], zr.at[c, d],
                 at(dh=d),
@@ -123,6 +124,9 @@
     arrived(RB.at[other], ks.at[1], kr.at[1])
     arrived(G.at[other], ks.at[2], kr.at[2])
 
+    def nearest(i):
+        return i + i // 2 - 2 * (i // 3)
+
     def to_x(c, yp):
         return copy(
             XS.at[c, yp], XR.at[c, x], xs.at[c, yp], xr.at[c, x],
@@ -155,7 +159,8 @@
         d = 1 if c % 2 == 0 else 3
         piece = A.at[c, y, (zh + 4 - d) % 4]
         arrived(piece, zs.at[c, d], zr.at[c, d])
-        send(piece, piece, zs.at[c, 2], zr.at[c, 2], at(dh=d))
+        if c >= DIRECT:
+            send(piece, piece, zs.at[c, 2], zr.at[c, 2], at(dh=d))
         if c + AHEAD < PARTS:
             attention_out(c + AHEAD)
 
@@ -168,7 +173,8 @@
 
     def project(c):
         @pl.loop(1, 4)
-        def _(d):
+        def _(i):
+            d = nearest(i)
             yp = (y + 4 - d) % 4
             arrived(A.at[c, yp], ys.at[c, d], yr.at[c, d])
             project_block(c, yp)
@@ -302,11 +308,12 @@
 
     def gram_part(c):
         arrived(CS.at[c], gs.at[c], gr.at[c])
-        for d in range(4):
-            arrived(R.at[other, c, (y + 4 - d) % 4], fs.at[c, d], fr.at[c, d])
 
         @pl.loop(0, 4)
-        def _(f):
+        def _(i):
+            d = nearest(i)
+            f = (y + 4 - d) % 4
+            arrived(R.at[other, c, f], fs.at[c, d], fr.at[c, d])
             start = pl.multiple_of(f * 256, 256)
             rows = pl.ds(start, 256)
             for half in range(2):

time: 130 us -> 128 us (0.985); the launches traced: 128 us -> 128 us
  no operation moved by 1% of the time
where the time goes in v4:
time: 128 us
  Pallas kernels  121 us (95%)
  local copies, waits for them, and re-layouts  5.68 us (4%)
    pallas_call x1, Pallas kernels, local(): pl.pallas_call(kernel, out_shape=(jax.ShapeDtypeStruct((128, 512), BF16),...  121 us
    unnamed x10, local copies, waits for them, and re-layouts  5.68 us

profile of v4, /device:TPU:1, one launch (start us, length us, event | category | flops | bytes accessed | tf_op | source)
XLA Modules:
  0.0 127.7 jit_solution(4247802883073485099)
XLA Ops:
  0.6 0.0 copy-start
  0.6 1.2 copy-done
  1.9 0.0 copy-start.1
  1.9 0.9 copy-done.1
  2.8 0.0 copy-start.2
  2.8 0.9 copy-done.2
  3.7 0.0 copy-start.3
  3.7 0.7 copy-done.3
  4.3 121.3 %shard_map.59 = (bf16[128,512]{1,0:T(8,128)(2,1)S(1)}, f32[1024,512]{1,0:T(8,128)S(1)}) custom-call(bf16[64,1024]{1,0:T(8,128)(2,1)S(1)} %copy-done.1, bf16[1024,512]{1,0:T(8,128)(2,1)S(1)} %copy-done, bf16[128,512]{1,0:T(8,128)(2,1)S(1)} %copy-done.2, f32[1,512]{1,0:T(1,128)S(1)} %bitcast.1), custom_call_target="tpu_custom_call" | custom-call | flops 4294967296 | bytes 16777216 | tf_op jit(solution)/shard_map/pallas_call | solution.py:374
  125.7 0.7 copy.8
  126.3 1.3 %copy.9 = f32[1024,512]{1,0:T(8,128)} copy(f32[1024,512]{1,0:T(8,128)S(1)} %get-tuple-element.5) | data formatting | bytes 4194304
Async XLA Ops:
  0.6 1.2 copy-start
  1.9 0.9 copy-start.1
  2.8 0.9 copy-start.2
  3.7 0.7 copy-start.3

commit v5 on v4

--- a/solution.py
+++ b/solution.py
@@ -14,7 +14,7 @@
 PARTS = 4
 T = 64 // PARTS
 AHEAD = 2
-DIRECT = 1
+DIRECT = 2
 STEPS = (
     ("attention_z", 39, 4), ("attention_y", 43, 4.5), ("project", 51, 5),
     ("combine", 60, 5), ("squares", 65, 5), ("norm", 72, 5), ("rows_z", 77, 5),

time: 128 us -> 134 us (1.047)
  the two profiles are of different devices: /device:TPU:1 before, /device:TPU:65 now
where the time goes in v5:
time: 134 us
  Pallas kernels  128 us (96%)
  local copies, waits for them, and re-layouts  5.68 us (4%)
    pallas_call x1, Pallas kernels, local(): pl.pallas_call(kernel, out_shape=(jax.ShapeDtypeStruct((128, 512), BF16),...  128 us
    unnamed x10, local copies, waits for them, and re-layouts  5.68 us

profile of v5, /device:TPU:65, one launch (start us, length us, event | category | flops | bytes accessed | tf_op | source)
XLA Modules:
  0.0 134.2 jit_solution(12428580003667079997)
XLA Ops:
  0.6 0.0 copy-start
  0.6 1.2 copy-done
  1.9 0.0 copy-start.1
  1.9 0.9 copy-done.1
  2.8 0.0 copy-start.2
  2.8 0.9 copy-done.2
  3.7 0.0 copy-start.3
  3.7 0.7 copy-done.3
  4.3 127.8 %shard_map.59 = (bf16[128,512]{1,0:T(8,128)(2,1)S(1)}, f32[1024,512]{1,0:T(8,128)S(1)}) custom-call(bf16[64,1024]{1,0:T(8,128)(2,1)S(1)} %copy-done.1, bf16[1024,512]{1,0:T(8,128)(2,1)S(1)} %copy-done, bf16[128,512]{1,0:T(8,128)(2,1)S(1)} %copy-done.2, f32[1,512]{1,0:T(1,128)S(1)} %bitcast.1), custom_call_target="tpu_custom_call" | custom-call | flops 4294967296 | bytes 16777216 | tf_op jit(solution)/shard_map/pallas_call | solution.py:374
  132.2 0.7 copy.8
  132.8 1.3 copy.9
Async XLA Ops:
  0.6 1.2 copy-start
  1.9 0.9 copy-start.1
  2.8 0.9 copy-start.2
  3.7 0.7 copy-start.3
